TPU v7x, 32 devices: a whole 2x2x4 slice. The times are simulated.
32 devices in a mesh: dap: 32 (over z, y, x, core), rep: 1.
Axes of the slice: x: 2, y: 2, z: 4, core: 2. Of those that a mesh axis runs over, the one named last changes fastest.
Arguments:
- pair_rep: bfloat16 [640, 640, 128], P(('rep', 'dap')), may hold values from -6 to 6
- token_mask: int32 [640], P('rep'), may hold values 0 or 1
- norm_gain: float32 [128], replicated, may hold values from 0.1 to 1.9
- norm_bias: float32 [128], replicated, may hold values from -1.5 to 1.5
- w_query: bfloat16 [128, 128], replicated, may hold values from -1 to 1
- w_key: bfloat16 [128, 128], replicated, may hold values from -0.5 to 0.5
- w_value: bfloat16 [128, 128], replicated, may hold values from -0.5 to 0.5
- w_gate: bfloat16 [128, 128], replicated, may hold values from -0.5 to 0.5
- gate_bias: float32 [128], replicated, may hold values from -4 to 4
- w_bias: bfloat16 [128, 4], replicated, may hold values from -0.5 to 0.5
- w_out: bfloat16 [128, 128], replicated, may hold values from -1.5 to 1.5
Outputs:
- update: bfloat16 [640, 640, 128], P(('rep', 'dap'))
Inputs may be any that keep to these rules, and one draw needn't show every extreme that they name: `token_mask`: 1 marks a valid token, 0 a padding token.
All inputs are finite; a program needn't handle non-finite values.
Results may differ from a plain program's by a relative error of at most 0.012.
Values may be sent and summed in bfloat16 or wider, within the bound.
A program may use at most 128 MiB of HBM per device.

v0:
```python
import jax
import jax.numpy as jnp
from jax import lax
from jax.sharding import PartitionSpec as P


def normalize(block, norm_gain, norm_bias):
    widened = block.astype(jnp.float32)
    average = jnp.mean(widened, axis=-1, keepdims=True)
    centred = widened - average
    variance = jnp.mean(centred * centred, axis=-1, keepdims=True)
    return (centred * lax.rsqrt(variance + 1e-05) * norm_gain + norm_bias).astype(jnp.bfloat16)


def project_all(normed, w_query, w_key, w_value, w_gate, gate_bias, q_scale):
    query_proj = (jnp.dot(normed, w_query, preferred_element_type=jnp.float32) * q_scale).astype(
        jnp.bfloat16
    )
    key_proj = jnp.dot(normed, w_key, preferred_element_type=jnp.float32).astype(jnp.bfloat16)
    value_proj = jnp.dot(normed, w_value, preferred_element_type=jnp.float32).astype(jnp.bfloat16)
    gate_proj = jax.nn.sigmoid(
        jnp.dot(normed, w_gate, preferred_element_type=jnp.float32) + gate_bias
    ).astype(jnp.bfloat16)
    return (query_proj, key_proj, value_proj, gate_proj)


def attend_column(column_inputs, bias_full, key_valid, head_count):
    query_col, key_col, value_col, gate_col, col_valid = column_inputs
    crop_len = query_col.shape[0]
    query_heads = query_col.reshape(crop_len, head_count, -1)
    key_heads = key_col.reshape(crop_len, head_count, -1)
    value_heads = value_col.reshape(crop_len, head_count, -1)
    scores = jnp.einsum("ihd,khd->hik", query_heads, key_heads, preferred_element_type=jnp.float32)
    scores = scores + bias_full.astype(jnp.float32)
    allowed = key_valid * col_valid > 0
    scores = jnp.where(allowed[None, None, :], scores, -1000000000.0)
    largest = jnp.max(scores, axis=-1, keepdims=True)
    weights = jnp.exp(scores - largest)
    attn_probs = (weights / jnp.sum(weights, axis=-1, keepdims=True)).astype(jnp.bfloat16)
    mixed_out = jnp.einsum(
        "hik,khd->ihd", attn_probs, value_heads, preferred_element_type=jnp.float32
    )
    mixed_out = mixed_out.reshape(crop_len, -1)
    return (mixed_out * gate_col.astype(jnp.float32)).astype(jnp.bfloat16)


def local(
    pair_rep,
    token_mask,
    norm_gain,
    norm_bias,
    w_query,
    w_key,
    w_value,
    w_gate,
    gate_bias,
    w_bias,
    w_out,
):
    row_count = pair_rep.shape[0]
    head_count = w_bias.shape[1]
    head_dim = w_query.shape[1] // head_count
    q_scale = head_dim ** (-0.5)
    normed = normalize(pair_rep, norm_gain, norm_bias)
    query_proj, key_proj, value_proj, gate_proj = project_all(
        normed, w_query, w_key, w_value, w_gate, gate_bias, q_scale
    )
    bias_proj = jnp.dot(normed, w_bias, preferred_element_type=jnp.float32).astype(jnp.bfloat16)
    bias_full = lax.all_gather(jnp.transpose(bias_proj, (2, 1, 0)), "dap", axis=2, tiled=True)
    query_proj, key_proj, value_proj, gate_proj = (
        lax.all_to_all(query_proj, "dap", split_axis=1, concat_axis=0, tiled=True),
        lax.all_to_all(key_proj, "dap", split_axis=1, concat_axis=0, tiled=True),
        lax.all_to_all(value_proj, "dap", split_axis=1, concat_axis=0, tiled=True),
        lax.all_to_all(gate_proj, "dap", split_axis=1, concat_axis=0, tiled=True),
    )
    offset = lax.axis_index("dap") * row_count
    col_valid = lax.dynamic_slice_in_dim(token_mask, offset, row_count)

    def one_column(column_inputs):
        return attend_column(column_inputs, bias_full, token_mask, head_count)

    gated_out = lax.map(
        one_column,
        (
            jnp.transpose(query_proj, (1, 0, 2)),
            jnp.transpose(key_proj, (1, 0, 2)),
            jnp.transpose(value_proj, (1, 0, 2)),
            jnp.transpose(gate_proj, (1, 0, 2)),
            col_valid,
        ),
    )
    gated_out = jnp.transpose(gated_out, (1, 0, 2))
    gated_back = lax.all_to_all(gated_out, "dap", split_axis=0, concat_axis=1, tiled=True)
    return jnp.dot(gated_back, w_out, preferred_element_type=jnp.float32).astype(jnp.bfloat16)


def solution(mesh):
    return jax.shard_map(
        local,
        mesh=mesh,
        in_specs=(
            P(("rep", "dap"), None, None),
            P("rep"),
            P(),
            P(),
            P(),
            P(),
            P(),
            P(),
            P(),
            P(),
            P(),
        ),
        out_specs=P(("rep", "dap"), None, None),
        check_vma=False,
    )
```

profile of v0, /device:TPU:0, one launch (start us, length us, event | category | flops | bytes accessed | tf_op | source)
XLA Modules:
  0.0 816.5 jit_solution(18252879614947546871)
XLA Ops:
  13.5 5.4 convolution_convert_fusion.2
  23.1 7.4 all-to-all-start
  30.5 5.5 multiply_convert_fusion
  40.1 78.7 %all-to-all-done = bf16[20,640,128]{2,0,1:T(8,128)(2,1)} async-done(((bf16[20,640,128]{2,0,1:T(8,128)(2,1)}), bf16[20,640,128]{2,0,1:T(8,128)(2,1)}, u32[]{:S(2)}, u32[]{:S(2)}) %all-to-all-start) | async-done | bytes 3276832 | tf_op jit(solution)/shard_map/all_to_all | solution.py:73
  122.9 5.4 convolution_convert_fusion.1
  132.4 78.7 %all-to-all-done.1 = bf16[20,640,128]{2,0,1:T(8,128)(2,1)} async-done(((bf16[20,640,128]{2,0,1:T(8,128)(2,1)}), bf16[20,640,128]{2,0,1:T(8,128)(2,1)}, u32[]{:S(2)}, u32[]{:S(2)}) %all-to-all-start.1) | async-done | bytes 3276832 | tf_op jit(solution)/shard_map/all_to_all | solution.py:71
  215.5 6.2 fusion.18
  221.7 5.7 divide_convert_fusion.2
  231.5 87.3 %all-to-all-done.2 = bf16[20,640,128]{2,0,1:T(8,128)(2,1)} async-done(((bf16[20,640,128]{2,0,1:T(8,128)(2,1)}), bf16[20,640,128]{2,0,1:T(8,128)(2,1)}, u32[]{:S(2)}, u32[]{:S(2)}) %all-to-all-start.2) | async-done | bytes 3276832 | tf_op jit(solution)/shard_map/all_to_all | solution.py:72
  327.2 5.1 copy.34
  332.3 6.2 all_to_all.68
  338.5 5.1 copy.37
  343.6 6.2 all_to_all.72
  349.8 5.1 copy.40
  354.9 6.2 all_to_all.76
  361.1 50.2 %all-to-all-done.3 = bf16[20,640,128]{2,0,1:T(8,128)(2,1)} async-done(((bf16[20,640,128]{2,0,1:T(8,128)(2,1)}), bf16[20,640,128]{2,0,1:T(8,128)(2,1)}, u32[]{:S(2)}, u32[]{:S(2)}) %all-to-all-start.3) | async-done | bytes 3276832 | tf_op jit(solution)/shard_map/all_to_all | solution.py:74
  411.3 5.0 copy.43
  416.4 6.2 all_to_all.80
  422.6 278.2 %while.10 = (s32[]{:T(128)}, bf16[20,640,128]{1,2,0:T(8,128)(2,1)}, bf16[20,640,128]{2,1,0:T(8,128)(2,1)}, s32[20]{0:T(128)S(1)}, s32[640]{0:T(1024)S(1)}, /*ind...) while((s32[]{:T(128)}, bf16[20,640,128]{1,2,0:T(8,128)(2,1)}, ...), condition=%wide.region_5.6_spmd, body=%wide.region_2.5_spmd.sunk | while | flops 332846080 | bytes 11002877 | solution.py:82
  426.2 4.4 fusion.49
  430.8 4.8 fusion.50
  440.1 4.4 fusion.49
  444.7 4.8 fusion.50
  454.0 4.4 fusion.49
  458.6 4.8 fusion.50
  467.9 4.4 fusion.49
  472.5 4.8 fusion.50
  481.8 4.4 fusion.49
  486.4 4.8 fusion.50
  495.8 4.4 fusion.49
  500.3 4.8 fusion.50
  514.3 4.8 fusion.50
  528.2 4.8 fusion.50
  542.1 4.8 fusion.50
  556.0 4.8 fusion.50
  569.9 4.8 fusion.50
  583.8 4.8 fusion.50
  597.7 4.8 fusion.50
  611.6 4.8 fusion.50
  625.5 4.8 fusion.50
  639.5 4.8 fusion.50
  653.4 4.8 fusion.50
  667.3 4.8 fusion.50
  681.2 4.8 fusion.50
  695.1 4.8 fusion.50
  700.8 6.2 copy.49
  707.1 92.2 %all_to_all.90 = bf16[640,20,128]{2,1,0:T(8,128)(2,1)S(1)} all-to-all(bf16[640,20,128]{2,1,0:T(8,128)(2,1)} %bitcast.87), channel_id=1, replica_groups=mesh['dap'=32,'rep'=1] {'dap'}, dimensions={0} | all-to-all | bytes 6553600 | tf_op jit(solution)/shard_map/all_to_all | solution.py:93
  802.2 4.7 all_to_all.84
  (237 shorter events, 200.3 us)
Async XLA Ops:
  6.5 6.9 copy-start
  6.5 3.0 copy-start.2
  6.5 6.9 copy-start.10
  6.5 6.9 copy-start.9
  23.1 7.4 copy-start.5
  23.1 95.7 %all-to-all-start = ((bf16[20,640,128]{2,0,1:T(8,128)(2,1)}), bf16[20,640,128]{2,0,1:T(8,128)(2,1)}, u32[]{:S(2)}, u32[]{:S(2)}) async-start(bf16[20,640,128]{2,0,1:T(8,128)(2,1)} %copy.32), calls=%async_computation | async-start | bytes 7864320 | tf_op jit(solution)/shard_map/all_to_all | solution.py:73
  40.1 82.8 %copy-start.6 = (bf16[128,128]{1,0:T(8,128)(2,1)S(1)}, bf16[128,128]{1,0:T(8,128)(2,1)}, u32[]{:S(2)}) copy-start(bf16[128,128]{1,0:T(8,128)(2,1)} %param.18) | copy-start | bytes 98308
  118.8 92.4 %all-to-all-start.1 = ((bf16[20,640,128]{2,0,1:T(8,128)(2,1)}), bf16[20,640,128]{2,0,1:T(8,128)(2,1)}, u32[]{:S(2)}, u32[]{:S(2)}) async-start(bf16[20,640,128]{2,0,1:T(8,128)(2,1)} %copy.35), calls=%async_computation.1 | async-start | bytes 7864320 | tf_op jit(solution)/shard_map/all_to_all | solution.py:71
  132.4 83.1 %copy-start.8 = (bf16[128,4]{0,1:T(4,128)(2,1)S(1)}, bf16[128,4]{0,1:T(4,128)(2,1)}, u32[]{:S(2)}) copy-start(bf16[128,4]{0,1:T(4,128)(2,1)} %param.22) | copy-start | bytes 3076
  211.1 107.7 %all-to-all-start.2 = ((bf16[20,640,128]{2,0,1:T(8,128)(2,1)}), bf16[20,640,128]{2,0,1:T(8,128)(2,1)}, u32[]{:S(2)}, u32[]{:S(2)}) async-start(bf16[20,640,128]{2,0,1:T(8,128)(2,1)} %copy.38), calls=%async_computation.2 | async-start | bytes 7864320 | tf_op jit(solution)/shard_map/all_to_all | solution.py:72
  215.3 6.5 copy-start.7
  215.3 6.5 copy-start.11
  215.3 107.9 %all-gather.2.cloned.1.call-start = ((), (), s32[]{:S(2)}) async-start(), calls=%async_computation.5 | async-start | bytes 3379200 | tf_op jit(solution)/shard_map/all_gather | solution.py:69
  231.5 91.6 %copy-start.3 = (s32[640]{0:T(1024)S(1)}, s32[640]{0:T(1024)}, u32[]{:S(2)}) copy-start(s32[640]{0:T(1024)} %param.14) | copy-start | bytes 7684
  318.8 92.5 %all-to-all-start.3 = ((bf16[20,640,128]{2,0,1:T(8,128)(2,1)}), bf16[20,640,128]{2,0,1:T(8,128)(2,1)}, u32[]{:S(2)}, u32[]{:S(2)}) async-start(bf16[20,640,128]{2,0,1:T(8,128)(2,1)} %copy.41), calls=%async_computation.3 | async-start | bytes 7864320 | tf_op jit(solution)/shard_map/all_to_all | solution.py:74
  802.2 4.7 copy-start.4
  802.2 7.5 copy-start.1
Sparse Core Ops, SparseCore 0:
  221.8 83.2 all-gather.1
where the time goes:
time: 820 us; the launch traced here: 817 us
  waiting for transfers between devices  295 us (36%)
  matrix products  216 us (26%)
  local copies, waits for them, and re-layouts  146 us (18%)
  blocking collectives  92.2 us (11%)
  other arithmetic  33.1 us (4%)
  starting transfers between devices  20.1 us (2%)
  between operations  13.6 us (2%)
    dot_general x20, matrix products, attend_column(): jnp.einsum('hik,khd->ihd', attn_probs, value_heads, preferred_element_typ...  96.8 us
    all_to_all x1, blocking collectives, local(): lax.all_to_all(gated_out, 'dap', split_axis=0, concat_axis=1, tiled=True)  92.2 us
    sub x20, matrix products, attend_column(): weights = jnp.exp(scores - largest)  88.5 us
    all_to_all x1, waiting for transfers between devices, local(): lax.all_to_all(key_proj, 'dap', split_axis=1, concat_axis=0, tiled=True)  87.3 us
    all_to_all x1, waiting for transfers between devices, local(): lax.all_to_all(query_proj, 'dap', split_axis=1, concat_axis=0, tiled=True)  78.7 us
    all_to_all x1, waiting for transfers between devices, local(): lax.all_to_all(value_proj, 'dap', split_axis=1, concat_axis=0, tiled=True)  78.7 us
    dynamic_slice x140, local copies, waits for them, and re-layouts, local(): lax.map(one_column, (jnp.transpose(query_proj, (1, 0, 2)), jnp.transpose(...  66.3 us
    all_to_all x1, waiting for transfers between devices, local(): lax.all_to_all(gate_proj, 'dap', split_axis=1, concat_axis=0, tiled=True)  50.2 us
  transfers between devices with their start and end apart: 5, of which 4 were waited for; matrix products, arithmetic and copies ran while one was open for 7% of the time, Pallas kernels for 0%

commit v1 on v0

v1 whole, which is shorter than its diff:
```python
import functools

import jax
import jax.numpy as jnp
from jax import lax
from jax.experimental import pallas as pl
from jax.experimental.pallas import tpu as pltpu
from jax.sharding import PartitionSpec as P

LOG2E = 1.4426950408889634
TILE = 256
SAFE = 70.0
BIG = 1e30


def normalize(block, norm_gain, norm_bias):
    widened = block.astype(jnp.float32)
    average = jnp.mean(widened, axis=-1, keepdims=True)
    centred = widened - average
    variance = jnp.mean(centred * centred, axis=-1, keepdims=True)
    return (centred * lax.rsqrt(variance + 1e-05) * norm_gain + norm_bias).astype(jnp.bfloat16)


def attend_kernel(
    heads,
    head_dim,
    q_scale,
    chunk,
    mask_ref,
    x_ref,
    gain_ref,
    nbias_ref,
    wq_ref,
    wqt_ref,
    wkt_ref,
    wv_ref,
    wg_ref,
    gbias_ref,
    wo_ref,
    bias_ref,
    kmask_ref,
    live_ref,
    out_ref,
    npad,
    q_buf,
    gate_buf,
    right,
    vext,
    probs,
    top_bias,
):
    step = pl.program_id(0)
    crop = x_ref.shape[1]
    slots = npad.shape[0]
    tiles = slots // TILE
    per = TILE - head_dim
    f32, bf16 = jnp.float32, jnp.bfloat16

    @pl.when(step == 0)
    def _():
        npad[...] = jnp.zeros_like(npad)
        r = lax.broadcasted_iota(jnp.int32, (TILE, TILE), 0)
        n = lax.broadcasted_iota(jnp.int32, (TILE, TILE), 1)
        eye = jnp.where(r == n + head_dim, 1.0, 0.0).astype(bf16)
        for h in range(heads):
            for t in range(tiles):
                right[h, t] = eye
        largest = jnp.zeros((1, 1), f32)
        for h in range(heads):
            largest = jnp.maximum(
                largest, jnp.max(jnp.abs(bias_ref[h].astype(f32)), keepdims=True)
            )
        top_bias[0] = largest[0, 0]

    normed = normalize(x_ref[0], gain_ref[...], nbias_ref[...])
    for t in range(tiles):
        count = min(per, crop - t * per)
        npad[t * TILE : t * TILE + count, :] = normed[t * per : t * per + count, :]
    q_buf[...] = (
        jnp.dot(normed, wq_ref[...], preferred_element_type=f32) * q_scale
    ).astype(bf16)
    gate_buf[...] = jax.nn.sigmoid(
        jnp.dot(normed, wg_ref[...], preferred_element_type=f32) + gbias_ref[...]
    ).astype(bf16)
    nt = (((1,), (1,)), ((), ()))
    padded = npad[...]
    key_t = lax.dot_general(wkt_ref[...], padded, nt, preferred_element_type=f32).astype(bf16)
    query_t = (
        lax.dot_general(wqt_ref[...], normed, nt, preferred_element_type=f32) * q_scale
    ).astype(bf16)
    value = jnp.dot(padded, wv_ref[...], preferred_element_type=f32).astype(bf16)

    bound = jnp.zeros((1, 1), f32)
    lanes = lax.broadcasted_iota(jnp.int32, (slots, heads * head_dim), 1)
    col_on = mask_ref[step] > 0
    kept = jnp.where(col_on, kmask_ref[...].astype(f32), live_ref[...].astype(f32)).astype(bf16)
    zero = jnp.zeros_like(kept)
    value = value * kept
    for h in range(heads):
        rows = slice(h * head_dim, (h + 1) * head_dim)
        k_h = key_t[rows, :]
        q_h = query_t[rows, :]
        for t in range(tiles):
            right[h, t, 0:head_dim, :] = k_h[:, t * TILE : (t + 1) * TILE]
        k2 = jnp.max(
            jnp.sum(jnp.square(k_h.astype(f32)), axis=0, keepdims=True), axis=1, keepdims=True
        )
        q2 = jnp.max(
            jnp.sum(jnp.square(q_h.astype(f32)), axis=0, keepdims=True), axis=1, keepdims=True
        )
        bound = jnp.maximum(bound, k2 * q2)
        mine = (lanes >= h * head_dim) & (lanes < (h + 1) * head_dim)
        vext[h * slots : (h + 1) * slots, 0 : heads * head_dim] = jnp.where(mine, value, zero)
        vext[h * slots : (h + 1) * slots, heads * head_dim : 2 * heads * head_dim] = jnp.where(
            mine, kept, zero
        )
    bound = jnp.sqrt(bound[0, 0]) + top_bias[0]
    safe = bound < SAFE
    scale = jnp.where(col_on, LOG2E, 0.0)

    def scores_of(r0, h, t):
        half = TILE // 2
        first = bias_ref[h, pl.ds(r0, chunk), t * TILE : t * TILE + half]
        first = first + q_buf[pl.ds(r0, chunk), h * half : (h + 1) * half]
        second = bias_ref[h, pl.ds(r0, chunk), t * TILE + half : (t + 1) * TILE]
        left = jnp.concatenate([first, second], axis=1)
        return jnp.dot(left, right[h, t], preferred_element_type=f32)

    def finish(r0):
        mixed = jnp.dot(probs[...], vext[...], preferred_element_type=f32)
        width = heads * head_dim
        gated = mixed[:, :width] / mixed[:, width:]
        gated = (gated * gate_buf[pl.ds(r0, chunk), :].astype(f32)).astype(bf16)
        out_ref[0, pl.ds(r0, chunk), :] = jnp.dot(
            gated, wo_ref[...], preferred_element_type=f32
        ).astype(bf16)

    @pl.when(safe)
    def _():
        @pl.loop(0, crop // chunk)
        def _(c):
            r0 = pl.multiple_of(c * chunk, chunk)
            for h in range(heads):
                for t in range(tiles):
                    s = scores_of(r0, h, t) * scale
                    probs[:, (h * tiles + t) * TILE : (h * tiles + t + 1) * TILE] = jnp.exp2(
                        s
                    ).astype(bf16)
            finish(r0)

    @pl.when(jnp.logical_not(safe))
    def _():
        ones = jnp.ones((chunk, heads * head_dim), bf16)

        @pl.loop(0, crop // chunk)
        def _(c):
            r0 = pl.multiple_of(c * chunk, chunk)
            for h in range(heads):
                held = []
                for t in range(tiles):
                    s = scores_of(r0, h, t) * scale
                    on = lax.dot_general(
                        ones,
                        kept[t * TILE : (t + 1) * TILE, :],
                        nt,
                        preferred_element_type=f32,
                    )
                    held.append(jnp.where(on > 0.0, s, -BIG))
                most = held[0].max(axis=1, keepdims=True)
                for t in range(1, tiles):
                    most = jnp.maximum(most, held[t].max(axis=1, keepdims=True))
                for t in range(tiles):
                    probs[:, (h * tiles + t) * TILE : (h * tiles + t + 1) * TILE] = jnp.exp2(
                        held[t] - most
                    ).astype(bf16)
            finish(r0)


def attend(x_cols, col_valid, gain, nbias, w_query, w_key, w_value, w_gate, gate_bias, w_out, bias_ext, kmask, live, heads):
    cols, crop, channels = x_cols.shape
    width = w_query.shape[1]
    head_dim = width // heads
    slots = bias_ext.shape[2]
    tiles = slots // TILE
    half = TILE // 2
    chunk = 160 if crop % 160 == 0 else crop
    wq_pad = jnp.pad(
        w_query.reshape(channels, heads, head_dim), ((0, 0), (0, 0), (0, half - head_dim))
    ).reshape(channels, heads * half)
    whole = lambda a: pl.BlockSpec(a.shape, lambda j, *_: (0,) * a.ndim)
    operands = (
        x_cols,
        gain.reshape(1, -1),
        nbias.reshape(1, -1),
        wq_pad,
        w_query.T,
        w_key.T,
        w_value,
        w_gate,
        gate_bias.reshape(1, -1),
        w_out,
        bias_ext,
        kmask,
        live,
    )
    specs = [pl.BlockSpec((1, crop, channels), lambda j, *_: (j, 0, 0))]
    specs += [whole(a) for a in operands[1:]]
    return pl.pallas_call(
        functools.partial(attend_kernel, heads, head_dim, head_dim ** (-0.5), chunk),
        out_shape=jax.ShapeDtypeStruct((cols, crop, w_out.shape[1]), jnp.bfloat16),
        grid_spec=pltpu.PrefetchScalarGridSpec(
            num_scalar_prefetch=1,
            grid=(cols,),
            in_specs=specs,
            out_specs=pl.BlockSpec((1, crop, w_out.shape[1]), lambda j, *_: (j, 0, 0)),
            scratch_shapes=[
                pltpu.VMEM((slots, channels), jnp.bfloat16),
                pltpu.VMEM((crop, heads * half), jnp.bfloat16),
                pltpu.VMEM((crop, width), jnp.bfloat16),
                pltpu.VMEM((heads, tiles, TILE, TILE), jnp.bfloat16),
                pltpu.VMEM((heads * slots, 2 * width), jnp.bfloat16),
                pltpu.VMEM((chunk, heads * slots), jnp.bfloat16),
                pltpu.SMEM((1,), jnp.float32),
            ],
        ),
        compiler_params=pltpu.CompilerParams(vmem_limit_bytes=48 * 1024 * 1024),
    )(col_valid, *operands)


def local(
    pair_rep,
    token_mask,
    norm_gain,
    norm_bias,
    w_query,
    w_key,
    w_value,
    w_gate,
    gate_bias,
    w_bias,
    w_out,
):
    rows, crop, channels = pair_rep.shape
    heads = w_bias.shape[1]
    head_dim = w_query.shape[1] // heads
    per = TILE - head_dim
    tiles = -(-crop // per)

    x_cols = lax.all_to_all(pair_rep, "dap", split_axis=1, concat_axis=0, tiled=True)
    x_cols = jnp.transpose(x_cols, (1, 0, 2))

    normed = normalize(pair_rep, norm_gain, norm_bias)
    bias_proj = jnp.dot(normed, w_bias, preferred_element_type=jnp.float32).astype(jnp.bfloat16)
    bias_full = lax.all_gather(jnp.transpose(bias_proj, (0, 2, 1)), "dap", axis=0, tiled=True)
    bias_full = jnp.transpose(bias_full, (1, 2, 0))
    bias_ext = jnp.pad(bias_full, ((0, 0), (0, 0), (0, tiles * per - crop)))
    bias_ext = bias_ext.reshape(heads, crop, tiles, per)
    bias_ext = jnp.pad(bias_ext, ((0, 0), (0, 0), (0, 0), (head_dim, 0)))
    bias_ext = bias_ext.reshape(heads, crop, tiles * TILE)

    def slotted(v):
        v = jnp.pad(v, (0, tiles * per - crop)).reshape(tiles, per)
        v = jnp.pad(v, ((0, 0), (0, TILE - per))).reshape(-1)
        return jnp.broadcast_to(v[:, None], (tiles * TILE, w_query.shape[1])).astype(jnp.bfloat16)

    offset = lax.axis_index("dap") * rows
    col_valid = lax.dynamic_slice_in_dim(token_mask, offset, rows)
    out_cols = attend(
        x_cols, col_valid, norm_gain, norm_bias, w_query, w_key, w_value, w_gate, gate_bias, w_out,
        bias_ext, slotted(token_mask), slotted(jnp.ones_like(token_mask)), heads,
    )
    return lax.all_to_all(
        jnp.transpose(out_cols, (1, 0, 2)), "dap", split_axis=0, concat_axis=1, tiled=True
    )


def solution(mesh):
    return jax.shard_map(
        local,
        mesh=mesh,
        in_specs=(
            P(("rep", "dap"), None, None),
            P("rep"),
            P(),
            P(),
            P(),
            P(),
            P(),
            P(),
            P(),
            P(),
            P(),
        ),
        out_specs=P(("rep", "dap"), None, None),
        check_vma=False,
    )
```

time: 820 us -> 357 us (0.44)
  matrix products: 216 us -> 6.18 us
  waiting for transfers between devices: 295 us -> 91.3 us
  local copies, waits for them, and re-layouts: 146 us -> 39.1 us
  Pallas kernels: 0 us -> 101 us
  other arithmetic: 33.1 us -> 6.94 us
  starting transfers between devices: 20.1 us -> 7.62 us
    all_to_all x4 -> x1, waiting for transfers between devices: 295 us -> 15.7 us  [local(): lax.all_to_all(pair_rep, 'dap', split_axis=1, concat_axis=0, tiled=True)]
    dot_general x25 -> x0, matrix products: 122 us -> none  [the longest x20 96.8 us: attend_column(): jnp.einsum('hik,khd->ihd', attn_probs, value_heads, preferred_element_typ...]
    pallas_call x0 -> x1, Pallas kernels: none -> 101 us  [attend(): pl.pallas_call(functools.partial(attend_kernel, heads, head_dim, head_dim...]
    sub x20 -> x0, matrix products: 88.5 us -> none  [attend_column(): weights = jnp.exp(scores - largest)]
    all_gather x1, waiting for transfers between devices: 0.01 us -> 75.6 us  [local(): lax.all_gather(jnp.transpose(bias_proj, (0, 2, 1)), 'dap', axis=0, tiled=...]
    dynamic_slice x141 -> x1, local copies, waits for them, and re-layouts: 66.4 us -> 0.08 us  [local(): col_valid = lax.dynamic_slice_in_dim(token_mask, offset, rows)]
    all_to_all x10 -> x4, local copies, waits for them, and re-layouts: 52.8 us -> 20.4 us  [the longest x2 11.3 us: local(): lax.all_to_all(pair_rep, 'dap', split_axis=1, concat_axis=0, tiled=True)]
    convert_element_type x4 -> x2, local copies, waits for them, and re-layouts: 16.4 us -> 0.04 us  [slotted(): jnp.broadcast_to(v[:, None], (tiles * TILE, w_query.shape[1]))]
  transfers between devices with their start and end apart: 5 -> 2, of which waited for: 4 -> 2; matrix products, arithmetic and copies ran while one was open for 7% -> 5% of each run, Pallas kernels for 0% -> 0%
where the time goes in v1:
time: 357 us
  Pallas kernels  101 us (28%)
  waiting for transfers between devices  91.3 us (26%)
  blocking collectives  91.3 us (26%)
  local copies, waits for them, and re-layouts  39.1 us (11%)
  between operations  13.6 us (4%)
  starting transfers between devices  7.62 us (2%)
  other arithmetic  6.94 us (2%)
  matrix products  6.18 us (2%)
    pallas_call x1, Pallas kernels, attend(): pl.pallas_call(functools.partial(attend_kernel, heads, head_dim, head_dim...  101 us
    all_to_all x1, blocking collectives, local(): lax.all_to_all(jnp.transpose(out_cols, (1, 0, 2)), 'dap', split_axis=0, c...  91.3 us
    all_gather x1, waiting for transfers between devices, local(): lax.all_gather(jnp.transpose(bias_proj, (0, 2, 1)), 'dap', axis=0, tiled=...  75.6 us
    all_to_all x1, waiting for transfers between devices, local(): lax.all_to_all(pair_rep, 'dap', split_axis=1, concat_axis=0, tiled=True)  15.7 us
    all_to_all x2, local copies, waits for them, and re-layouts, local(): lax.all_to_all(pair_rep, 'dap', split_axis=1, concat_axis=0, tiled=True)  11.3 us
    all_to_all x2, local copies, waits for them, and re-layouts, local(): lax.all_to_all(jnp.transpose(out_cols, (1, 0, 2)), 'dap', split_axis=0, c...  9.13 us
    all_to_all x1, starting transfers between devices, local(): lax.all_to_all(pair_rep, 'dap', split_axis=1, concat_axis=0, tiled=True)  7.59 us
  transfers between devices with their start and end apart: 2, of which 2 were waited for; matrix products, arithmetic and copies ran while one was open for 5% of the time, Pallas kernels for 0%

profile of v1, /device:TPU:0, one launch (start us, length us, event | category | flops | bytes accessed | tf_op | source)
XLA Modules:
  0.0 356.7 jit_solution(12114762605965565324)
XLA Ops:
  6.5 0.0 copy-start
  6.5 0.0 copy-start.7
  6.5 0.0 copy-start.4
  6.5 0.0 copy-start.5
  6.5 0.0 all-gather.2.cloned.1.call-start
  6.6 3.0 convert_reduce_fusion
  9.6 0.0 copy-done.7
  9.6 3.9 %fusion.2 = f32[20,640]{1,0:T(8,128)S(1)} fusion(bf16[20,640,128]{2,1,0:T(8,128)(2,1)S(1)} %copy-done.7, f32[20,640]{1,0:T(8,128)S(1)} %broadcast_multiply_fusion), kind=kLoop, calls=%fused_computation.4 | loop fusion | flops 6540800 | bytes 3379200 | tf_op jit(solution)/shard_map/reduce_sum | solution.py:20
  13.6 0.0 copy-done
  13.6 0.0 copy-done.4
  13.6 0.0 copy-done.5
  13.6 6.2 %fusion.11 = bf16[20,4,640]{2,1,0:T(4,128)(2,1)} fusion(bf16[20,640,128]{2,1,0:T(8,128)(2,1)S(1)} %copy-done.7, f32[128]{0:T(128)S(1)} %copy-done.5, f32[128]{0:T(128)S(1)} %copy-done.4, f32[20,640]{1,0:T(8,128)S(1)} %add_rsqrt_fusion, f32[20,640]{1,0:T(8,128)S(1)} %broadcast_multiply_fusion, bf16[128,4]{0,1:T(4,128)(2,1)S(1)} %copy-done), kind=kOutput, calls=%fused_computation.10 | convolution fusion | flops 22988800 | bytes 3483648 | tf_op jit(solution)/shard_map/dot_general | solution.py:253
  19.8 0.0 all-gather.2.cloned.1.call-update
  19.8 4.1 %copy.25 = bf16[20,640,128]{2,0,1:T(8,128)(2,1)} copy(bf16[20,640,128]{2,1,0:T(8,128)(2,1)S(1)} %copy-done.7) | data formatting | bytes 6553600 | tf_op args[0]
  23.9 0.0 copy-start.10
  23.9 0.0 copy-start.8
  23.9 0.0 copy-start.9
  23.9 7.6 %all-to-all-start = ((bf16[20,640,128]{2,0,1:T(8,128)(2,1)}), bf16[20,640,128]{2,0,1:T(8,128)(2,1)}, u32[]{:S(2)}, u32[]{:S(2)}) async-start(bf16[20,640,128]{2,0,1:T(8,128)(2,1)} %copy.25), calls=%async_computation | async-start | bytes 7864320 | tf_op jit(solution)/shard_map/all_to_all | solution.py:249
  31.5 0.0 copy-done.10
  31.5 0.1 dynamic_slice.3.mask_ref
  31.6 0.0 copy-done.8
  31.6 0.1 copy.28
  31.7 0.1 copy.39.wq_ref
  31.9 0.0 copy-done.9
  31.9 0.1 copy.31
  32.0 0.1 reshape.54
  32.1 0.1 reshape.55
  32.2 75.6 %all-gather.2.cloned.1.call-done = bf16[640,4,640]{2,1,0:T(4,128)(2,1)} async-done(((bf16[20,4,640]{2,1,0:T(4,128)(2,1)}), bf16[640,4,640]{2,1,0:T(4,128)(2,1)}) %all-gather.2.cloned.1.call-update) | async-done | bytes 3276816 | tf_op jit(solution)/shard_map/all_gather | solution.py:254
  107.8 2.3 copy.42
  110.2 0.3 pad.31.clone
  110.5 2.4 pad.32
  112.9 6.3 %copy.33.bias_ref = bf16[4,640,768]{2,1,0:T(8,128)(2,1)} copy(bf16[4,640,768]{1,2,0:T(8,128)(2,1)} %bitcast.35) | data formatting | bytes 7864320 | tf_op jit(solution)/shard_map/reshape | solution.py:259
  119.1 15.7 %all-to-all-done = bf16[20,640,128]{2,0,1:T(8,128)(2,1)} async-done(((bf16[20,640,128]{2,0,1:T(8,128)(2,1)}), bf16[20,640,128]{2,0,1:T(8,128)(2,1)}, u32[]{:S(2)}, u32[]{:S(2)}) %all-to-all-start) | async-done | bytes 3276832 | tf_op jit(solution)/shard_map/all_to_all | solution.py:249
  134.8 5.1 %copy.27 = bf16[32,20,20,128]{3,1,0,2:T(8,128)(2,1)} copy(bf16[32,20,20,128]{3,1,2,0:T(8,128)(2,1)} %bitcast.2) | data formatting | bytes 6553600 | tf_op jit(solution)/shard_map/all_to_all | solution.py:249
  139.9 0.0 copy-start.1
  139.9 0.0 copy-start.2
  139.9 6.3 %all_to_all.29 = bf16[640,20,128]{2,0,1:T(8,128)(2,1)} reshape(bf16[32,20,20,128]{3,1,0,2:T(8,128)(2,1)} %copy.27) | data formatting | bytes 6553600 | tf_op jit(solution)/shard_map/all_to_all | solution.py:249
  146.2 0.2 broadcast_in_dim.6.kmask_ref
  146.3 0.2 broadcast_in_dim.8.live_ref
  146.5 0.0 copy-done.1
  146.5 0.0 copy-done.2
  146.5 0.0 copy-done.3
  146.5 0.0 copy-done.6
  146.5 100.6 %shard_map.109 = bf16[20,640,128]{2,1,0:T(8,128)(2,1)S(1)} custom-call(s32[20]{0:T(128)S(1)} %dynamic_slice.3.mask_ref, bf16[20,640,128]{2,1,0:T(8,128)(2,1)} %bitcast.37, f32[1,128]{1,0:T(1,128)S(1)} %bitcast.31, f32[1,128]{1,0:T(1,128)S(1)} %bitcast.32, bf16[128,512]{1,0:T(8,128)(2,1)S(1)} %copy.39.wq_ref, bf16[128,128]{1,0:T(8,128)(2,1)S(1)} %bitcast.29, ...), custom_call_target="tpu_custom_call" | custom-call | tf_op jit(solution)/shard_map/pallas_call | solution.py:208
  247.1 2.2 copy.34
  249.3 91.3 %all_to_all.36 = bf16[640,20,128]{2,1,0:T(8,128)(2,1)S(1)} all-to-all(bf16[640,20,128]{2,1,0:T(8,128)(2,1)S(1)} %copy.34), channel_id=1, replica_groups=mesh['dap'=32,'rep'=1] {'dap'}, dimensions={0} | all-to-all | bytes 6553600 | tf_op jit(solution)/shard_map/all_to_all | solution.py:272
  340.7 2.9 copy.36
  343.6 6.2 %all_to_all.33 = bf16[20,640,128]{2,1,0:T(8,128)(2,1)} reshape(bf16[20,32,20,128]{3,2,1,0:T(8,128)(2,1)} %copy.36) | data formatting | bytes 6553600 | tf_op jit(solution)/shard_map/all_to_all | solution.py:272
  (13 shorter events, 0.1 us)
Async XLA Ops:
  6.5 7.0 %copy-start = (bf16[128,4]{0,1:T(4,128)(2,1)S(1)}, bf16[128,4]{0,1:T(4,128)(2,1)}, u32[]{:S(2)}) copy-start(bf16[128,4]{0,1:T(4,128)(2,1)} %param.20) | copy-start | bytes 3076
  6.5 3.1 copy-start.7
  6.5 7.0 %copy-start.4 = (f32[128]{0:T(128)S(1)}, f32[128]{0:T(128)}, u32[]{:S(2)}) copy-start(f32[128]{0:T(128)} %param.13) | copy-start | bytes 1540
  6.5 7.0 %copy-start.5 = (f32[128]{0:T(128)S(1)}, f32[128]{0:T(128)}, u32[]{:S(2)}) copy-start(f32[128]{0:T(128)} %param.14) | copy-start | bytes 1540
  6.5 101.3 %all-gather.2.cloned.1.call-start = ((), (), s32[]{:S(2)}) async-start(), calls=%async_computation.2 | async-start | bytes 3379200 | tf_op jit(solution)/shard_map/all_gather | solution.py:254
  23.9 7.6 %copy-start.10 = (s32[640]{0:T(1024)S(1)}, s32[640]{0:T(1024)}, u32[]{:S(2)}) copy-start(s32[640]{0:T(1024)} %param.12) | copy-start | bytes 7684
  23.9 7.7 %copy-start.8 = (bf16[128,128]{1,0:T(8,128)(2,1)S(1)}, bf16[128,128]{1,0:T(8,128)(2,1)}, u32[]{:S(2)}) copy-start(bf16[128,128]{1,0:T(8,128)(2,1)} %param.15) | copy-start | bytes 98308
  23.9 8.0 %copy-start.9 = (bf16[128,128]{1,0:T(8,128)(2,1)S(1)}, bf16[128,128]{1,0:T(8,128)(2,1)}, u32[]{:S(2)}) copy-start(bf16[128,128]{1,0:T(8,128)(2,1)} %param.16) | copy-start | bytes 98308
  23.9 111.0 %all-to-all-start = ((bf16[20,640,128]{2,0,1:T(8,128)(2,1)}), bf16[20,640,128]{2,0,1:T(8,128)(2,1)}, u32[]{:S(2)}, u32[]{:S(2)}) async-start(bf16[20,640,128]{2,0,1:T(8,128)(2,1)} %copy.25), calls=%async_computation | async-start | bytes 7864320 | tf_op jit(solution)/shard_map/all_to_all | solution.py:249
  139.9 6.6 %copy-start.1 = (bf16[128,128]{1,0:T(8,128)(2,1)S(1)}, bf16[128,128]{1,0:T(8,128)(2,1)}, u32[]{:S(2)}) copy-start(bf16[128,128]{1,0:T(8,128)(2,1)} %wv_ref.1) | copy-start | bytes 98308
  139.9 6.6 %copy-start.2 = (bf16[128,128]{1,0:T(8,128)(2,1)S(1)}, bf16[128,128]{1,0:T(8,128)(2,1)}, u32[]{:S(2)}) copy-start(bf16[128,128]{1,0:T(8,128)(2,1)} %wg_ref.1) | copy-start | bytes 98308
  139.9 6.6 %copy-start.3 = (bf16[128,128]{1,0:T(8,128)(2,1)S(1)}, bf16[128,128]{1,0:T(8,128)(2,1)}, u32[]{:S(2)}) copy-start(bf16[128,128]{1,0:T(8,128)(2,1)} %wo_ref.1) | copy-start | bytes 98308
  139.9 6.6 %copy-start.6 = (f32[128]{0:T(128)S(1)}, f32[128]{0:T(128)}, u32[]{:S(2)}) copy-start(f32[128]{0:T(128)} %param.19) | copy-start | bytes 1540
Sparse Core Ops, SparseCore 0:
  19.9 87.8 all-gather.1
